TPU v7x, 1024 devices: a whole 4x8x16 slice. The times are simulated.
1024 devices in a mesh: rep: 16 (over x, y_hi), exp: 64 (over y_lo, z, core).
Axes of the slice: x: 4, y: 8 (y_hi: 4, y_lo: 2; y = y_hi * 2 + y_lo), z: 16, core: 2. Of those that a mesh axis runs over, the one named last changes fastest.
Arguments:
- quant_rows: bfloat16 [32768, 2048], P(('rep', 'exp')), may hold values from -6 to 6
- row_scales: bfloat16 [32768], P(('rep', 'exp')), may hold values from 0.29882812 to 3
- out_grads: bfloat16 [32768, 2048], P(('rep', 'exp')), may hold values from -6 to 6
- routes: int32 [32768, 4], P(('rep', 'exp')), may hold values from 0 to 63, all different within a row; in each aligned block of 32 rows (0 to 31, 32 to 63, ...) at most 4 rows name the same one
- probs: bfloat16 [32768, 4], P(('rep', 'exp')), may hold values from 0.099609375 to 1
- w_gate: bfloat16 [64, 2048, 768], P('exp'), may hold values from -0.125 to 0.125
- w_up: bfloat16 [64, 2048, 768], P('exp'), may hold values from -0.125 to 0.125
- w_down: bfloat16 [64, 768, 2048], P('exp'), may hold values from -0.21875 to 0.21875
Outputs:
- input_grads: bfloat16 [32768, 2048], P(('rep', 'exp'))
- grad_gate: bfloat16 [64, 2048, 768], P('exp', 'rep')
- grad_up: bfloat16 [64, 2048, 768], P('exp', 'rep')
Inputs may be any that keep to these rules, and one draw needn't show every extreme that they name: `routes`: each token names 4 different experts; among the tokens of one device no expert is named more than 4 times, a bound that some block reaches.
All inputs are finite; a program needn't handle non-finite values.
Results may differ from a plain program's by a relative error of at most 0.018.
Values may be sent and summed in bfloat16 or wider, within the bound.
A program may use at most 128 MiB of HBM per device.

v0:
```python
import jax
import jax.numpy as jnp
from jax import lax
from jax.sharding import PartitionSpec as P


def swiglu_backward(gate_proj, up_proj, grad_hidden):
    sigmoid_gate = jax.nn.sigmoid(gate_proj)
    act_slope = sigmoid_gate * (1.0 + gate_proj * (1.0 - sigmoid_gate))
    gate_grad = (grad_hidden * up_proj * act_slope).astype(jnp.bfloat16)
    up_grad = (grad_hidden * gate_proj * sigmoid_gate).astype(jnp.bfloat16)
    return (gate_grad, up_grad)


def body(quant_rows, row_scales, out_grads, routes, probs, w_gate, w_up, w_down):
    tok_count = quant_rows.shape[0]
    model_width = quant_rows.shape[1]
    top_count = routes.shape[1]
    local_experts = w_gate.shape[0]
    hidden = w_gate.shape[2]
    owners = lax.axis_size("exp")
    experts = owners * local_experts
    capacity = max(2, 2 * tok_count * top_count // experts)
    slot_count = experts * capacity
    route_count = tok_count * top_count
    flat_routes = routes.reshape(-1)
    chosen = (flat_routes[:, None] == jnp.arange(experts, dtype=jnp.int32)[None, :]).astype(
        jnp.int32
    )
    earlier = jnp.cumsum(chosen, axis=0) - chosen
    slot_rank = jnp.sum(earlier * chosen, axis=1)
    target = flat_routes * capacity + slot_rank
    slot_route = (
        jnp.full((slot_count,), -1, jnp.int32)
        .at[target]
        .set(jnp.arange(route_count, dtype=jnp.int32))
    )
    slot_valid = slot_route >= 0
    safe_route = jnp.maximum(slot_route, 0)
    slot_token = safe_route // top_count
    zero_row = jnp.zeros((), jnp.bfloat16)
    sent_rows = jnp.where(slot_valid[:, None], quant_rows[slot_token], zero_row)
    sent_grads = jnp.where(slot_valid[:, None], out_grads[slot_token], zero_row)
    sent_small = jnp.stack([row_scales[slot_token], probs.reshape(-1)[safe_route]], axis=1)
    sent_small = jnp.where(slot_valid[:, None], sent_small, zero_row)
    got_rows, got_grads, got_small = (
        lax.all_to_all(
            sent_rows.reshape(experts, capacity, model_width),
            "exp",
            split_axis=0,
            concat_axis=0,
            tiled=True,
        ),
        lax.all_to_all(
            sent_grads.reshape(experts, capacity, model_width),
            "exp",
            split_axis=0,
            concat_axis=0,
            tiled=True,
        ),
        lax.all_to_all(
            sent_small.reshape(experts, capacity, 2), "exp", split_axis=0, concat_axis=0, tiled=True
        ),
    )
    rows_in = got_rows.reshape(owners, local_experts, capacity, model_width)
    grads_in = got_grads.reshape(owners, local_experts, capacity, model_width)
    small_in = got_small.reshape(owners, local_experts, capacity, 2).astype(jnp.float32)
    scale_in = small_in[:, :, :, 0:1]
    prob_in = small_in[:, :, :, 1:2]
    gate_proj = (
        jnp.einsum("secd,edf->secf", rows_in, w_gate, preferred_element_type=jnp.float32) * scale_in
    )
    up_proj = (
        jnp.einsum("secd,edf->secf", rows_in, w_up, preferred_element_type=jnp.float32) * scale_in
    )
    grad_hidden = (
        jnp.einsum("secd,efd->secf", grads_in, w_down, preferred_element_type=jnp.float32) * prob_in
    )
    gate_grad, up_grad = swiglu_backward(gate_proj, up_proj, grad_hidden)
    row_grads = jnp.einsum("secf,edf->secd", gate_grad, w_gate, preferred_element_type=jnp.float32)
    row_grads = (
        row_grads + jnp.einsum("secf,edf->secd", up_grad, w_up, preferred_element_type=jnp.float32)
    ).astype(jnp.bfloat16)
    scaled_rows = (rows_in.astype(jnp.float32) * scale_in).astype(jnp.bfloat16)
    both_grads = jnp.concatenate([gate_grad, up_grad], axis=3)
    returned = lax.all_to_all(
        row_grads.reshape(experts, capacity, model_width),
        "exp",
        split_axis=0,
        concat_axis=0,
        tiled=True,
    )
    route_rows = returned.reshape(slot_count, model_width)[target]
    summed_rows = jnp.sum(
        route_rows.reshape(tok_count, top_count, model_width).astype(jnp.float32), axis=1
    )
    input_grads = summed_rows.astype(jnp.bfloat16)
    width_first = jnp.transpose(scaled_rows, (3, 1, 0, 2)).reshape(
        model_width, local_experts, owners * capacity
    )
    grads_first = jnp.transpose(both_grads, (1, 0, 2, 3)).reshape(
        local_experts, owners * capacity, 2 * hidden
    )
    summed = lax.psum_scatter(
        jnp.einsum(
            "dex,exf->def", width_first, grads_first, preferred_element_type=jnp.float32
        ).astype(jnp.bfloat16),
        "rep",
        scatter_dimension=0,
        tiled=True,
    ).astype(jnp.float32)
    summed = jnp.transpose(summed, (1, 0, 2))
    weights_out = summed.astype(jnp.bfloat16)
    return (input_grads, weights_out[:, :, :hidden], weights_out[:, :, hidden:])


def solution(mesh):
    in_specs = (
        P(("rep", "exp"), None),
        P(("rep", "exp")),
        P(("rep", "exp"), None),
        P(("rep", "exp"), None),
        P(("rep", "exp"), None),
        P("exp", None, None),
        P("exp", None, None),
        P("exp", None, None),
    )
    out_specs = (P(("rep", "exp"), None), P("exp", "rep", None), P("exp", "rep", None))
    return jax.shard_map(body, mesh=mesh, in_specs=in_specs, out_specs=out_specs, check_vma=False)
```

profile of v0, /device:TPU:6, one launch (start us, length us, event | category | flops | bytes accessed | tf_op | source)
XLA Modules:
  0.0 363.2 jit_solution(2133679599965813675)
XLA Ops:
  7.2 0.0 copy-start
  7.2 1.8 fusion.66
  9.0 2.1 fusion.65
  11.1 0.7 broadcast_multiply_fusion
  11.8 0.8 copy.48
  12.6 0.1 copy.47
  12.6 0.1 mul.83
  12.8 0.1 eq.15
  12.9 0.1 fusion.59
  13.0 0.2 reduce_window_sum.11
  13.1 0.2 select_reduce_fusion
  13.3 1.0 scatter_custom_fusion
  14.3 0.8 copy.51
  15.1 0.1 reshape.138
  15.2 0.1 broadcast_in_dim.48
  15.4 0.1 copy.50
  15.5 1.9 gather_fusion.1
  17.3 0.1 stack.10
  17.5 0.1 copy.53
  17.5 20.1 %compare_select_fusion.2 = bf16[256]{0:T(256)(128)(2,1)S(1)} fusion(bf16[]{:T(256)} %bitcast.6, bf16[]{:T(256)} %bitcast.7, bf16[]{:T(256)} %bitcast.8, bf16[]{:T(256)} %bitcast.9, bf16[]{:T(256)} %bitcast.10, bf16[]{:T(256)} %bitcast.11, bf16[]{:T(256)} %bitcast.12, bf16[]{:T(256)} %bitcast.13, bf16[]{:T(256)} %bitcast.14, bf16[]{:T(256)} %bitcast.15, ...), kind=kLoop, calls=%fused_computation.53 | loop fusion | flops 18944 | bytes 1600 | tf_op jit(solution)/shard_map/gather | solution.py:44
  37.6 0.1 stack.9
  37.8 0.1 copy.52
  37.9 0.7 copy.54
  38.6 20.8 %all-to-all-start.1 = ((bf16[64,4,2]{1,2,0:T(2,128)(2,1)}), bf16[64,4,2]{1,2,0:T(2,128)(2,1)S(1)}, u32[]{:S(2)}, u32[]{:S(2)}) async-start(bf16[64,4,2]{1,2,0:T(2,128)(2,1)} %copy.54), calls=%async_computation.1 | async-start | bytes 65536 | tf_op jit(solution)/shard_map/all_to_all | solution.py:61
  59.4 2.4 gather_fusion.2
  61.8 2.3 gather.24
  64.1 2.4 gather_fusion
  66.4 2.2 gather.20
  68.6 3.9 %broadcast_select_fusion = (bf16[64,4,2048]{2,1,0:T(4,128)(2,1)}, bf16[64,4,2048]{2,1,0:T(4,128)(2,1)}) fusion(bf16[64,4,2048]{2,1,0:T(4,128)(2,1)} %gather.24, pred[64,4]{1,0:T(8,128)(4,1)S(1)} %broadcast_in_dim.48, bf16[64,4,2048]{2,1,0:T(4,128)(2,1)} %gather.20), kind=kLoop, calls=%fused_computation.34 | loop fusion | flops 1048576 | bytes 4194560 | tf_op jit(solution)/shard_map/jit(_where)/select_n | solution.py:42
  72.5 0.2 all-to-all-done.1
  72.7 65.8 %all_to_all.20 = bf16[64,4,2048]{2,1,0:T(4,128)(2,1)} all-to-all(bf16[64,4,2048]{2,1,0:T(4,128)(2,1)} %get-tuple-element.19), channel_id=1, replica_groups=mesh['rep'=16,'exp'=64] {'exp'}, dimensions={0} | all-to-all | bytes 2097152 | tf_op jit(solution)/shard_map/all_to_all | solution.py:47
  138.6 8.0 %all-to-all-start = ((bf16[64,4,2048]{2,1,0:T(4,128)(2,1)}), bf16[64,4,2048]{2,1,0:T(4,128)(2,1)}, u32[]{:S(2)}, u32[]{:S(2)}) async-start(bf16[64,4,2048]{2,1,0:T(4,128)(2,1)} %get-tuple-element.20), calls=%async_computation | async-start | bytes 2097152 | tf_op jit(solution)/shard_map/all_to_all | solution.py:54
  146.6 0.0 reduce-scatter.4.cloned.1.call-start
  146.7 0.1 fusion.64
  146.7 0.1 copy.55
  146.8 0.1 copy.57
  146.9 2.7 fusion.53
  149.6 2.1 reshape.146
  151.7 4.0 %fusion.29 = f32[64,1,4,768]{3,0,2,1:T(8,128)} fusion(bf16[1,2048,768]{2,1,0:T(8,128)(2,1)S(1)} %copy-done, bf16[64,4,2048]{2,1,0:T(4,128)(2,1)} %all_to_all.20, f32[64,4]{0,1:T(4,128)S(1)} %copy.57), kind=kOutput, calls=%fused_computation.24 | convolution fusion | flops 805502976 | bytes 4981760 | tf_op jit(solution)/shard_map/secd,edf->secf/dot_general | solution.py:71
  155.7 43.0 %all-to-all-done = bf16[64,4,2048]{2,1,0:T(4,128)(2,1)} async-done(((bf16[64,4,2048]{2,1,0:T(4,128)(2,1)}), bf16[64,4,2048]{2,1,0:T(4,128)(2,1)}, u32[]{:S(2)}, u32[]{:S(2)}) %all-to-all-start) | async-done | bytes 1048608 | tf_op jit(solution)/shard_map/all_to_all | solution.py:54
  198.7 4.5 %multiply_convert_fusion.1 = (bf16[64,1,4,768]{3,0,2,1:T(8,128)(2,1)S(1)}, f32[64,1,4,768]{3,0,2,1:T(8,128)S(1)}) fusion(f32[64,1,4,768]{3,0,2,1:T(8,128)} %fusion.29, f32[64,4]{0,1:T(4,128)S(1)} %copy.55, bf16[1,768,2048]{2,1,0:T(8,128)(2,1)} %param.15, bf16[64,4,2048]{2,1,0:T(4,128)(2,1)} %all-to-all-done), kind=kOutput, calls=%fused_computation.39 | convolution fusion | flops 806682624 | bytes 6161408 | tf_op jit(solution)/shard_map/secd,efd->secf/dot_general | solution.py:77
  203.3 2.0 fusion.50
  205.3 0.1 pad_maximum_fusion
  205.4 0.7 copy-done.8
  206.1 1.5 copy.60
  207.6 2.3 reshape.145
  209.9 5.9 %fusion = bf16[2048,1536]{0,1:T(8,128)(2,1)} fusion(bf16[256,1536]{1,0:T(8,128)(2,1)} %reshape.145, bf16[2048,256]{0,1:T(8,128)(2,1)} %reshape.146), kind=kOutput, calls=%fused_computation.6 | convolution fusion | flops 1613758464 | bytes 8126464 | tf_op jit(solution)/shard_map/dex,exf->def/dot_general | solution.py:105
  215.8 8.6 %copy.65 = bf16[2048,1536]{1,0:T(8,128)(2,1)} copy(bf16[2048,1536]{0,1:T(8,128)(2,1)} %fusion) | data formatting | bytes 12582912
  224.5 0.0 reduce-scatter.4.cloned.1.call-update
  224.5 0.0 copy-start.5
  224.5 2.2 fusion.1
  226.7 1.0 fusion.14
  227.7 1.8 copy.59
  229.5 8.0 %all-to-all-start.3 = ((bf16[64,4,2048]{2,1,0:T(4,128)(2,1)}), bf16[64,4,2048]{2,1,0:T(4,128)(2,1)}, u32[]{:S(2)}, u32[]{:S(2)}) async-start(bf16[64,4,2048]{2,1,0:T(4,128)(2,1)} %copy.59), calls=%async_computation.3 | async-start | bytes 2097152 | tf_op jit(solution)/shard_map/all_to_all | solution.py:86
  237.6 52.1 %all-to-all-done.3 = bf16[64,4,2048]{2,1,0:T(4,128)(2,1)} async-done(((bf16[64,4,2048]{2,1,0:T(4,128)(2,1)}), bf16[64,4,2048]{2,1,0:T(4,128)(2,1)}, u32[]{:S(2)}, u32[]{:S(2)}) %all-to-all-start.3) | async-done | bytes 1048608 | tf_op jit(solution)/shard_map/all_to_all | solution.py:86
  289.7 2.2 reshape.143
  291.8 3.6 gather_fusion.3
  295.5 2.0 reshape.144
  297.5 2.3 reduce_sum.25
  299.8 50.3 %reduce-scatter.4.cloned.1.call-done = bf16[128,1536]{1,0:T(8,128)(2,1)} async-done(((bf16[2048,1536]{1,0:T(8,128)(2,1)}), bf16[128,1536]{1,0:T(8,128)(2,1)}) %reduce-scatter.4.cloned.1.call-update) | async-done | bytes 393232
  350.1 1.9 copy.66
  352.0 1.7 fusion.63
  353.8 1.7 copy.62
  355.5 0.8 copy.61
  (25 shorter events, 0.1 us)
Async XLA Ops:
  7.2 144.5 %copy-start = (bf16[1,2048,768]{2,1,0:T(8,128)(2,1)S(1)}, bf16[1,2048,768]{2,1,0:T(8,128)(2,1)}, u32[]{:S(2)}) copy-start(bf16[1,2048,768]{2,1,0:T(8,128)(2,1)} %param.13) | copy-start | bytes 9437188
  7.2 52.2 %copy-start.1 = (bf16[32,2048]{1,0:T(8,128)(2,1)S(1)}, bf16[32,2048]{1,0:T(8,128)(2,1)}, u32[]{:S(2)}) copy-start(bf16[32,2048]{1,0:T(8,128)(2,1)} %param.8) | copy-start | bytes 393220
  38.6 34.1 %all-to-all-start.1 = ((bf16[64,4,2]{1,2,0:T(2,128)(2,1)}), bf16[64,4,2]{1,2,0:T(2,128)(2,1)S(1)}, u32[]{:S(2)}, u32[]{:S(2)}) async-start(bf16[64,4,2]{1,2,0:T(2,128)(2,1)} %copy.54), calls=%async_computation.1 | async-start | bytes 65536 | tf_op jit(solution)/shard_map/all_to_all | solution.py:61
  61.8 2.3 copy-start.2
  138.6 60.1 %all-to-all-start = ((bf16[64,4,2048]{2,1,0:T(4,128)(2,1)}), bf16[64,4,2048]{2,1,0:T(4,128)(2,1)}, u32[]{:S(2)}, u32[]{:S(2)}) async-start(bf16[64,4,2048]{2,1,0:T(4,128)(2,1)} %get-tuple-element.20), calls=%async_computation | async-start | bytes 2097152 | tf_op jit(solution)/shard_map/all_to_all | solution.py:54
  146.6 203.5 %reduce-scatter.4.cloned.1.call-start = ((), (), s32[]{:S(2)}) async-start(), calls=%async_computation.5 | async-start | bytes 6684672
  198.7 4.6 %copy-start.3 = (bf16[64,4,2048]{2,1,0:T(4,128)(2,1)S(1)}, bf16[64,4,2048]{2,1,0:T(4,128)(2,1)}, u32[]{:S(2)}) copy-start(bf16[64,4,2048]{2,1,0:T(4,128)(2,1)} %all_to_all.20) | copy-start | bytes 3145732
  198.7 4.6 %copy-start.4 = (bf16[1,2048,768]{2,1,0:T(8,128)(2,1)S(1)}, bf16[1,2048,768]{2,1,0:T(8,128)(2,1)}, u32[]{:S(2)}) copy-start(bf16[1,2048,768]{2,1,0:T(8,128)(2,1)} %param.14) | copy-start | bytes 9437188
  198.7 4.6 %copy-start.9 = (f32[64,1,4,768]{3,0,2,1:T(8,128)S(1)}, f32[64,1,4,768]{3,0,2,1:T(8,128)}, u32[]{:S(2)}) copy-start(f32[64,1,4,768]{3,0,2,1:T(8,128)} %fusion.29) | copy-start | bytes 2359300
  203.2 2.1 copy-start.6
  205.3 0.8 copy-start.8
  224.5 2.2 copy-start.5
  224.5 2.2 copy-start.7
  229.5 60.1 %all-to-all-start.3 = ((bf16[64,4,2048]{2,1,0:T(4,128)(2,1)}), bf16[64,4,2048]{2,1,0:T(4,128)(2,1)}, u32[]{:S(2)}, u32[]{:S(2)}) async-start(bf16[64,4,2048]{2,1,0:T(4,128)(2,1)} %copy.59), calls=%async_computation.3 | async-start | bytes 2097152 | tf_op jit(solution)/shard_map/all_to_all | solution.py:86
Sparse Core Ops, SparseCore 0:
  224.6 125.4 reduce-scatter.3
where the time goes:
time: 365 us; the launch traced here: 363 us
  waiting for transfers between devices  146 us (40%)
  blocking collectives  65.8 us (18%)
  local copies, waits for them, and re-layouts  50.7 us (14%)
  starting transfers between devices  36.9 us (10%)
  other arithmetic  30.3 us (8%)
  matrix products  19.7 us (5%)
  between operations  14.3 us (4%)
    all_to_all x1, blocking collectives, body(): lax.all_to_all(sent_rows.reshape(experts, capacity, model_width), 'exp',...  65.8 us
    all_to_all x1, waiting for transfers between devices, body(): lax.all_to_all(row_grads.reshape(experts, capacity, model_width), 'exp',...  52.1 us
    unnamed x2, waiting for transfers between devices  50.3 us
    all_to_all x1, waiting for transfers between devices, body(): lax.all_to_all(sent_grads.reshape(experts, capacity, model_width), 'exp',...  43 us
    all_to_all x1, starting transfers between devices, body(): lax.all_to_all(sent_small.reshape(experts, capacity, 2), 'exp', split_axi...  20.8 us
    gather x1, other arithmetic, body(): row_scales[slot_token]  20.1 us
    unnamed x26, local copies, waits for them, and re-layouts  15.4 us
    all_to_all x1, starting transfers between devices, body(): lax.all_to_all(row_grads.reshape(experts, capacity, model_width), 'exp',...  8.02 us
  transfers between devices with their start and end apart: 4, of which 4 were waited for; matrix products, arithmetic and copies ran while one was open for 10% of the time, Pallas kernels for 0%

commit v1 on v0

v1 whole, which is shorter than its diff:
```python
import functools

import jax
import jax.numpy as jnp
from jax import lax
from jax.experimental import pallas as pl
from jax.experimental.pallas import tpu as pltpu
from jax.sharding import PartitionSpec as P

MESH = pl.DeviceIdType.MESH
F32 = jnp.float32
BF16 = jnp.bfloat16

NX, NYH, NZ, NC = 4, 4, 16, 2
NJ = 4
HALF = NZ // 2
CAP = 4
SUBS = 3


def kernel(
    x_ref, scale_ref, g_ref, routes_ref, probs_ref, wg_hbm, wu_hbm, wd_hbm,
    out_ref, gate_ref, up_ref,
    wg, wu, wd, meta, xs, gs, pm, stage, got, xt, both, rows_back, returned, yown,
    zsend, zrecv, dw, zed, recv1, recv2,
    w_sem, f_send, f_recv, p_send, p_recv, b_send, b_recv, z_send, z_recv, r_send, r_recv,
):
    tok, dim = x_ref.shape
    ff = wg.shape[1]
    tile = 256
    pieces = 2 * ff // tile
    rep, exp = lax.axis_index("rep"), lax.axis_index("exp")
    my_x, my_y = rep // NYH, rep % NYH
    y_lo, z, core = exp // (NZ * NC), exp // NC % NZ, exp % NC

    def z_dev(step):
        return (rep, y_lo * (NZ * NC) + (z + NZ + step) % NZ * NC + core)

    def plane_exp(j):
        other_y = 1 - y_lo if j // 2 else y_lo
        other_c = 1 - core if j % 2 else core
        return other_y * (NZ * NC) + z * NC + other_c

    def x_dev(step):
        return ((my_x + NX + step) % NX * NYH + my_y, exp)

    def y_dev(step):
        return (my_x * NYH + (my_y + NYH + step) % NYH, exp)

    weights = [
        pltpu.make_async_copy(src, dst, w_sem.at[i])
        for i, (src, dst) in enumerate(((wg_hbm, wg), (wu_hbm, wu), (wd_hbm, wd)))
    ]
    for copy in weights:
        copy.start()

    neighbours = [z_dev(1), z_dev(-1), x_dev(1), x_dev(-1), y_dev(1), y_dev(-1)]
    neighbours += [(rep, plane_exp(j)) for j in range(1, NJ)]
    barrier = pltpu.get_barrier_semaphore()
    for device in neighbours:
        pl.semaphore_signal(barrier, inc=1, device_id=device, device_id_type=MESH)

    def iota(shape, axis):
        return lax.broadcasted_iota(jnp.int32, shape, axis)

    diag = jnp.where(iota((tok, tok), 0) == iota((tok, tok), 1), scale_ref[...].astype(F32), 0.0)
    diag = diag.astype(BF16)
    xs[0] = jnp.dot(diag, x_ref[...], preferred_element_type=F32).astype(BF16)
    gs[0] = g_ref[...]
    lanes = NJ * tok
    spread = (iota((tok, lanes), 1) % tok == iota((tok, lanes), 0)).astype(BF16)
    over_tokens = (((0,), (0,)), ((), ()))
    table = lax.dot_general(
        routes_ref[...].astype(F32).astype(BF16), spread, over_tokens, preferred_element_type=F32
    )
    chance = lax.dot_general(probs_ref[...], spread, over_tokens, preferred_element_type=F32)
    experts = NJ * NZ
    hits = [iota((experts, lanes), 0).astype(F32) == table[k : k + 1] for k in range(4)]
    named = sum(hit.astype(F32) for hit in hits)
    a, b = iota((lanes, lanes), 0), iota((lanes, lanes), 1)
    before = ((a // tok == b // tok) & (a < b)).astype(BF16)
    rank = jnp.dot(named.astype(BF16), before, preferred_element_type=F32)
    for k in range(4):
        mine = jnp.sum(jnp.where(hits[k], rank, 0.0), axis=0, keepdims=True)
        meta[0, k : k + 1, :] = table[k : k + 1] * CAP + mine
        meta[0, 4 + k : 5 + k, :] = chance[k : k + 1]

    pl.semaphore_wait(barrier, len(neighbours))

    pending = []

    def remote(src, dst, send, recv, device):
        return pltpu.make_async_remote_copy(
            src_ref=src, dst_ref=dst, send_sem=send, recv_sem=recv,
            device_id=device, device_id_type=MESH,
        )

    travels = (meta, xs, gs)

    def slot_of(way, hop):
        return 0 if hop == 0 else 15 if hop == HALF else 2 * hop - 1 + way

    def carries(way, hop, sub):
        return hop < HALF or (sub == 2) == (way == 1)

    def hop_copy(way, hop, sub):
        buf = travels[sub]
        return remote(
            buf.at[slot_of(way, hop - 1)], buf.at[slot_of(way, hop)],
            f_send.at[way, hop - 1, sub], f_recv.at[way, hop - 1, sub],
            z_dev(1 if way == 0 else -1),
        )

    def hop_start(way, hop, sub):
        if hop <= HALF and carries(way, hop, sub):
            copy = hop_copy(way, hop, sub)
            copy.start()
            pending.append(copy)

    for sub in range(SUBS):
        for way in range(2):
            hop_start(way, 1, sub)

    group_rows = NJ * 4 * CAP
    r = iota((group_rows, lanes), 0)
    c = iota((group_rows, lanes), 1)
    expert_of = jnp.where(
        r // 16 == 0, plane_exp(0),
        jnp.where(r // 16 == 1, plane_exp(1), jnp.where(r // 16 == 2, plane_exp(2), plane_exp(3))),
    )
    slot_id = jnp.where(r % 16 // CAP == c // tok, expert_of * CAP + r % CAP, -1).astype(F32)

    def plane_copy(group, j, kind):
        return remote(
            stage.at[kind, group, j], got.at[kind, j, pl.ds(group * 16, 16)],
            p_send.at[group, j - 1, kind], p_recv.at[group, j - 1, kind], (rep, plane_exp(j)),
        )

    def select(group):
        lane_group = iota((8, lanes), 1) // tok
        mix = meta[group * 4]
        for m in range(1, 4):
            mix = jnp.where(lane_group == m, meta[group * 4 + m], mix)
        hit = [slot_id == mix[k : k + 1] for k in range(4)]
        ones = sum(h.astype(F32) for h in hit)
        pm[group] = ones.astype(BF16)
        weighed = sum(jnp.where(hit[k], mix[4 + k : 5 + k], 0.0) for k in range(4))
        picks = (pm[group], weighed.astype(BF16))
        for kind, buf in ((0, xs), (1, gs)):
            for n in range(0, dim, 512):
                block = buf[group * 4 : group * 4 + 4, :, n : n + 512].reshape(4 * tok, 512)
                chosen = jnp.dot(picks[kind], block, preferred_element_type=F32).astype(BF16)
                got[kind, 0, group * 16 : group * 16 + 16, n : n + 512] = chosen[:16]
                stage[kind, group, 1:, :, n : n + 512] = chosen[16:].reshape(3, 16, 512)
            for j in range(1, NJ):
                copy = plane_copy(group, j, kind)
                copy.start()
                pending.append(copy)

    for hop in range(1, HALF + 1):
        for sub in range(SUBS):
            for way in range(2):
                if carries(way, hop, sub):
                    hop_copy(way, hop, sub).wait_recv()
                    hop_start(way, hop + 1, sub)
        if hop % 2 == 0:
            select(hop // 2 - 1)

    for copy in weights:
        copy.wait()
    for group in range(4):
        for j in range(1, NJ):
            for kind in range(2):
                plane_copy(group, j, kind).wait_recv()

    slots = NJ * 64
    over_last = (((1,), (1,)), ((), ()))

    def project(f, carry):
        cols = pl.ds(pl.multiple_of(f * tile, tile), tile)
        ins = got[0].reshape(slots, dim)
        gate = jnp.dot(ins, wg[:, cols], preferred_element_type=F32)
        up = jnp.dot(ins, wu[:, cols], preferred_element_type=F32)
        grads = got[1].reshape(slots, dim)
        hidden = lax.dot_general(grads, wd[cols, :], over_last, preferred_element_type=F32)
        s = jax.nn.sigmoid(gate)
        both[f] = (hidden * up * s * (1.0 + gate * (1.0 - s))).astype(BF16)
        both[f + ff // tile] = (hidden * gate * s).astype(BF16)
        return carry

    lax.fori_loop(0, ff // tile, project, 0)

    def turn(n, carry):
        cols = pl.ds(pl.multiple_of(n * tile, tile), tile)
        xt[n] = got[0, :, :, cols].reshape(slots, tile).T
        return carry

    lax.fori_loop(0, dim // tile, turn, 0)

    axes = ((x_dev, y_dev), (y_dev, x_dev))
    order_of = [1 if p == 1 else 0 for p in range(pieces)]

    def weight_piece(p):
        order = order_of[p]

        def one(i, carry):
            value = jnp.dot(xt[i], both[p], preferred_element_type=F32).astype(BF16)
            rx = (i // 2 - my_x + NX) % NX
            for h in range(2):
                ry = (2 * (i % 2) + h - my_y + NYH) % NYH
                part = value[h * 128 : (h + 1) * 128]
                if order == 0:
                    dw[p, rx, ry] = part
                else:
                    dw[p, ry, rx] = part
            return carry

        lax.fori_loop(0, dim // tile, one, 0)

    def ring_copy(phase, p, way, m):
        to = axes[order_of[p]][phase](1 if way == 0 else -1)
        near = 1 if way == 0 else 3
        block = (2, near, near)[m]
        half = (way, 1 - way, way)[m]
        if phase == 0:
            src = dw.at[p, block, pl.ds(half * 2, 2)]
            dst = recv1.at[p, way, m]
        else:
            src = zed.at[p, block, pl.ds(half * 64, 64)]
            dst = recv2.at[p, way, m]
        return remote(src, dst, r_send.at[phase, p, way, m], r_recv.at[phase, p, way, m], to)

    def ring_start(phase, p, way, m):
        copy = ring_copy(phase, p, way, m)
        copy.start()
        pending.append(copy)

    def ring_first(phase, p):
        for m in range(2):
            for way in range(2):
                ring_start(phase, p, way, m)

    def ring_add(phase, p):
        for way in range(2):
            ring_copy(phase, p, way, 0).wait_recv()
            near = 1 if way == 0 else 3
            if phase == 0:
                for h in range(2):
                    dw[p, near, way * 2 + h] = (
                        dw[p, near, way * 2 + h].astype(F32) + recv1[p, way, 0, h].astype(F32)
                    ).astype(BF16)
            else:
                here = pl.ds(way * 64, 64)
                zed[p, near, here] = (
                    zed[p, near, here].astype(F32) + recv2[p, way, 0].astype(F32)
                ).astype(BF16)
            ring_start(phase, p, way, 2)

    def ring_end(phase, p):
        for way in range(2):
            for m in range(1, 3):
                ring_copy(phase, p, way, m).wait_recv()
        for half in range(2):
            low_m, high_m = (2, 1) if half == 0 else (1, 2)
            if phase == 0:
                for h in range(2):
                    total = dw[p, 0, half * 2 + h].astype(F32)
                    total += recv1[p, 0, low_m, h].astype(F32)
                    total += recv1[p, 1, high_m, h].astype(F32)
                    zed[p, half * 2 + h] = total.astype(BF16)
            else:
                here = pl.ds(half * 64, 64)
                total = zed[p, 0, here].astype(F32)
                total += recv2[p, 0, low_m].astype(F32)
                total += recv2[p, 1, high_m].astype(F32)
                target = gate_ref if p < pieces // 2 else up_ref
                q = p % (pieces // 2)
                target[here, q * tile : (q + 1) * tile] = total.astype(BF16)
        if phase == 0:
            ring_first(1, p)

    def back_copy(j):
        return remote(
            rows_back.at[j], returned.at[j], b_send.at[j - 1], b_recv.at[j - 1],
            (rep, plane_exp(j)),
        )

    def row_grads():
        def one(n, carry):
            cols = pl.ds(pl.multiple_of(n * tile, tile), tile)
            total = jnp.zeros((slots, tile), F32)
            for k in range(ff // tile):
                inner = slice(k * tile, (k + 1) * tile)
                total += lax.dot_general(
                    both[k], wg[cols, inner], over_last, preferred_element_type=F32
                )
                total += lax.dot_general(
                    both[k + ff // tile], wu[cols, inner], over_last, preferred_element_type=F32
                )
            value = total.astype(BF16).reshape(NJ, 64, tile)
            rows_back[:, :, cols] = value
            return carry

        lax.fori_loop(0, dim // tile, one, 0)
        for j in range(1, NJ):
            copy = back_copy(j)
            copy.start()
            pending.append(copy)

    def combine():
        for j in range(1, NJ):
            back_copy(j).wait_recv()
        for group in range(3, -1, -1):
            rows = pl.ds(group * 16, 16)
            for n in range(0, dim, 512):
                cols = slice(n, n + 512)
                parts = jnp.concatenate(
                    [rows_back[0, rows, cols]] + [returned[j, rows, cols] for j in range(1, NJ)], 0
                )
                sums = lax.dot_general(pm[group], parts, over_tokens, preferred_element_type=F32)
                yown[group * 4 : group * 4 + 4, :, cols] = sums.reshape(4, tok, 512)

    wide = dim // 2

    def line_copy(way, hop, half):
        return remote(
            zsend.at[way, hop - 1, half], zrecv.at[way, hop - 1, half],
            z_send.at[way, hop - 1, half], z_recv.at[way, hop - 1, half],
            z_dev(-1 if way == 0 else 1),
        )

    def line_start(way, hop, half):
        copy = line_copy(way, hop, half)
        copy.start()
        pending.append(copy)

    def line_far():
        for way in range(2):
            zsend[way, HALF - 1, way] = yown[15, :, way * wide : (way + 1) * wide].astype(BF16)
            line_start(way, HALF, way)

    def line_step(hop):
        halves = ((1, 0), (0, 1)) if hop == HALF - 1 else ((0, 1), (0, 1))
        for turn_ in range(2):
            for way in range(2):
                half = halves[way][turn_] if hop == HALF - 1 else turn_
                total = yown[slot_of(way, hop), :, half * wide : (half + 1) * wide]
                if hop < HALF - 1 or half == way:
                    line_copy(way, hop + 1, half).wait_recv()
                    total = total + zrecv[way, hop, half].astype(F32)
                zsend[way, hop - 1, half] = total.astype(BF16)
                line_start(way, hop, half)

    def line_end():
        for half in range(2):
            cols = slice(half * wide, (half + 1) * wide)
            total = yown[0, :, cols]
            for way in range(2):
                line_copy(way, 1, half).wait_recv()
                total = total + zrecv[way, 0, half].astype(F32)
            out_ref[:, cols] = total.astype(BF16)

    tasks = []
    weight_piece(0)
    ring_first(0, 0)
    weight_piece(1)
    ring_first(0, 1)
    row_grads()
    weight_piece(2)
    ring_first(0, 2)
    for p in range(3, pieces):
        weight_piece(p)

    x_pieces = [p for p in range(pieces) if order_of[p] == 0]
    y_pieces = [p for p in range(pieces) if order_of[p] == 1]

    def lot(p, follow):
        ring_add(0, p)
        if follow is not None:
            ring_first(0, follow)

    step = 7.9
    for i, p in enumerate(x_pieces):
        follow = x_pieces[i + 2] if i + 2 < len(x_pieces) else None
        tasks.append((step * i + 4, functools.partial(lot, p, follow)))
        tasks.append((step * (i + 1) + 2, functools.partial(ring_end, 0, p)))
        tasks.append((step * (i + 1) + 5, functools.partial(ring_add, 1, p)))
        tasks.append((step * (i + 1) + 9, functools.partial(ring_end, 1, p)))
    for i, p in enumerate(y_pieces):
        tasks.append((8.5, functools.partial(ring_add, 0, p)))
        tasks.append((24, functools.partial(ring_end, 0, p)))
        tasks.append((29, functools.partial(ring_add, 1, p)))
        tasks.append((33, functools.partial(ring_end, 1, p)))
    tasks.append((11, combine))
    tasks.append((11.1, line_far))
    for hop in range(HALF - 1, 0, -1):
        tasks.append((11.2 + 3.5 * (HALF - hop), functools.partial(line_step, hop)))
    tasks.append((11.2 + 3.5 * HALF, line_end))
    for _, task in sorted(tasks, key=lambda entry: entry[0]):
        task()
    for copy in pending:
        copy.wait_send()


def body(quant_rows, row_scales, out_grads, routes, probs, w_gate, w_up, w_down):
    tok, dim = quant_rows.shape
    ff = w_gate.shape[2]
    pieces = 2 * ff // 256
    vmem = pl.BlockSpec(memory_space=pltpu.VMEM)
    hbm = pl.BlockSpec(memory_space=pl.ANY)
    dma = pltpu.SemaphoreType.DMA
    wide = dim // 2
    out, gate, up = pl.pallas_call(
        kernel,
        out_shape=(
            jax.ShapeDtypeStruct((tok, dim), BF16),
            jax.ShapeDtypeStruct((128, ff), BF16),
            jax.ShapeDtypeStruct((128, ff), BF16),
        ),
        in_specs=[vmem] * 5 + [hbm] * 3,
        out_specs=(vmem, vmem, vmem),
        scratch_shapes=[
            pltpu.VMEM((dim, ff), BF16),
            pltpu.VMEM((dim, ff), BF16),
            pltpu.VMEM((ff, dim), BF16),
            pltpu.VMEM((NZ, 8, NJ * tok), F32),
            pltpu.VMEM((NZ, tok, dim), BF16),
            pltpu.VMEM((NZ, tok, dim), BF16),
            pltpu.VMEM((4, 64, NJ * tok), BF16),
            pltpu.VMEM((2, 4, NJ, 16, dim), BF16),
            pltpu.VMEM((2, NJ, 64, dim), BF16),
            pltpu.VMEM((dim // 256, 256, 256), BF16),
            pltpu.VMEM((pieces, 256, 256), BF16),
            pltpu.VMEM((NJ, 64, dim), BF16),
            pltpu.VMEM((NJ, 64, dim), BF16),
            pltpu.VMEM((NZ, tok, dim), F32),
            pltpu.VMEM((2, HALF, 2, tok, wide), BF16),
            pltpu.VMEM((2, HALF, 2, tok, wide), BF16),
            pltpu.VMEM((pieces, 4, 4, 128, 256), BF16),
            pltpu.VMEM((pieces, 4, 128, 256), BF16),
            pltpu.VMEM((pieces, 2, 3, 2, 128, 256), BF16),
            pltpu.VMEM((pieces, 2, 3, 64, 256), BF16),
            dma((3,)),
            dma((2, HALF, SUBS)),
            dma((2, HALF, SUBS)),
            dma((4, 3, 2)),
            dma((4, 3, 2)),
            dma((3,)),
            dma((3,)),
            dma((2, HALF, 2)),
            dma((2, HALF, 2)),
            dma((2, pieces, 2, 3)),
            dma((2, pieces, 2, 3)),
        ],
        compiler_params=pltpu.CompilerParams(
            collective_id=0, has_side_effects=True, vmem_limit_bytes=60 * 1024 * 1024
        ),
    )(
        quant_rows, row_scales.reshape(1, tok), out_grads, routes, probs,
        w_gate[0], w_up[0], w_down[0],
    )
    return out, gate[None], up[None]


def solution(mesh):
    in_specs = (
        P(("rep", "exp"), None),
        P(("rep", "exp")),
        P(("rep", "exp"), None),
        P(("rep", "exp"), None),
        P(("rep", "exp"), None),
        P("exp", None, None),
        P("exp", None, None),
        P("exp", None, None),
    )
    out_specs = (P(("rep", "exp"), None), P("exp", "rep", None), P("exp", "rep", None))
    return jax.shard_map(body, mesh=mesh, in_specs=in_specs, out_specs=out_specs, check_vma=False)
```

time: 365 us -> 167 us (0.46)
  Pallas kernels: 0 us -> 157 us
  waiting for transfers between devices: 146 us -> 0 us
  blocking collectives: 65.8 us -> 0 us
  local copies, waits for them, and re-layouts: 50.7 us -> 7.53 us
  starting transfers between devices: 36.9 us -> 0 us
  other arithmetic: 30.3 us -> 0 us
  matrix products: 19.7 us -> 0 us
  between operations: 14.3 us -> 0.64 us
    pallas_call x0 -> x1, Pallas kernels: none -> 157 us  [body(): pl.pallas_call(kernel, out_shape=(jax.ShapeDtypeStruct((tok, dim), BF16),...]
    all_to_all x3 -> x0, waiting for transfers between devices: 95.2 us -> none  [the longest x1 52.1 us: body(): lax.all_to_all(row_grads.reshape(experts, capacity, model_width), 'exp',...]
    all_to_all x1 -> x0, blocking collectives: 65.8 us -> none  [body(): lax.all_to_all(sent_rows.reshape(experts, capacity, model_width), 'exp',...]
    unnamed x2 -> x0, waiting for transfers between devices: 50.3 us -> none
    all_to_all x3 -> x0, starting transfers between devices: 36.8 us -> none  [the longest x1 20.8 us: body(): lax.all_to_all(sent_small.reshape(experts, capacity, 2), 'exp', split_axi...]
    gather x3 -> x0, other arithmetic: 20.1 us -> none  [the longest x1 20.1 us: body(): row_scales[slot_token]]
    dot_general x6 -> x0, matrix products: 19.7 us -> none  [the longest x1 5.93 us: body(): jnp.einsum('dex,exf->def', width_first, grads_first, preferred_element_ty...]
    gather x8 -> x0, local copies, waits for them, and re-layouts: 18.6 us -> none  [the longest x2 4.63 us: body(): sent_rows = jnp.where(slot_valid[:, None], quant_rows[slot_token], zero_row)]
  transfers between devices with their start and end apart: 4 -> 0, of which waited for: 4 -> 0; matrix products, arithmetic and copies ran while one was open for 10% -> 0% of each run, Pallas kernels for 0% -> 0%
where the time goes in v1:
time: 167 us; the launch traced here: 165 us
  Pallas kernels  157 us (94%)
  local copies, waits for them, and re-layouts  7.53 us (5%)
    pallas_call x1, Pallas kernels, body(): pl.pallas_call(kernel, out_shape=(jax.ShapeDtypeStruct((tok, dim), BF16),...  157 us
    unnamed x5, local copies, waits for them, and re-layouts  7.53 us

profile of v1, /device:TPU:6, one launch (start us, length us, event | category | flops | bytes accessed | tf_op | source)
XLA Modules:
  0.0 165.2 jit_solution(9951945051233984729)
XLA Ops:
  0.6 1.4 copy.12.probs_ref
  2.0 1.4 copy.11.routes_ref
  3.4 157.1 %shard_map.103 = (bf16[32,2048]{1,0:T(8,128)(2,1)}, bf16[128,768]{1,0:T(8,128)(2,1)}, bf16[128,768]{1,0:T(8,128)(2,1)}) custom-call(bf16[32,2048]{1,0:T(8,128)(2,1)} %x_ref.1, bf16[1,32]{1,0:T(2,128)(2,1)} %bitcast.11, bf16[32,2048]{1,0:T(8,128)(2,1)} %g_ref.1, s32[32,4]{1,0:T(8,128)} %copy.11.routes_ref, bf16[32,4]{1,0:T(8,128)(2,1)} %copy.12.probs_ref, ...), custom_call_target="tpu_custom_call" | custom-call | tf_op jit(solution)/shard_map/pallas_call | solution.py:413
  160.4 1.6 copy.16
  162.0 1.6 copy.17
  163.6 1.6 copy.18

commit v2 on v1

--- a/solution.py
+++ b/solution.py
@@ -70,10 +70,10 @@
     lanes = NJ * tok
     spread = (iota((tok, lanes), 1) % tok == iota((tok, lanes), 0)).astype(BF16)
     over_tokens = (((0,), (0,)), ((), ()))
-    table = lax.dot_general(
-        routes_ref[...].astype(F32).astype(BF16), spread, over_tokens, preferred_element_type=F32
+    table = jnp.dot(
+        routes_ref[...].astype(F32).astype(BF16), spread, preferred_element_type=F32
     )
-    chance = lax.dot_general(probs_ref[...], spread, over_tokens, preferred_element_type=F32)
+    chance = jnp.dot(probs_ref[...], spread, preferred_element_type=F32)
     experts = NJ * NZ
     hits = [iota((experts, lanes), 0).astype(F32) == table[k : k + 1] for k in range(4)]
     named = sum(hit.astype(F32) for hit in hits)
@@ -132,7 +132,7 @@
 
     def plane_copy(group, j, kind):
         return remote(
-            stage.at[kind, group, j], got.at[kind, j, pl.ds(group * 16, 16)],
+            stage.at[kind, group, j], got.at[kind, group, j],
             p_send.at[group, j - 1, kind], p_recv.at[group, j - 1, kind], (rep, plane_exp(j)),
         )
 
@@ -150,12 +150,72 @@
             for n in range(0, dim, 512):
                 block = buf[group * 4 : group * 4 + 4, :, n : n + 512].reshape(4 * tok, 512)
                 chosen = jnp.dot(picks[kind], block, preferred_element_type=F32).astype(BF16)
-                got[kind, 0, group * 16 : group * 16 + 16, n : n + 512] = chosen[:16]
+                got[kind, group, 0, :, n : n + 512] = chosen[:16]
                 stage[kind, group, 1:, :, n : n + 512] = chosen[16:].reshape(3, 16, 512)
             for j in range(1, NJ):
                 copy = plane_copy(group, j, kind)
                 copy.start()
                 pending.append(copy)
+
+    slots = NJ * 64
+    over_last = (((1,), (1,)), ((), ()))
+
+    def project(low, high):
+        for group in range(low, high):
+            for j in range(1, NJ):
+                for kind in range(2):
+                    plane_copy(group, j, kind).wait_recv()
+        here, count = slice(low * 64, high * 64), (high - low) * 64
+        for f in range(ff // tile):
+            cols = slice(f * tile, (f + 1) * tile)
+            ins = got[0, low:high].reshape(count, dim)
+            gate = jnp.dot(ins, wg[:, cols], preferred_element_type=F32)
+            up = jnp.dot(ins, wu[:, cols], preferred_element_type=F32)
+            grads = got[1, low:high].reshape(count, dim)
+            hidden = lax.dot_general(grads, wd[cols, :], over_last, preferred_element_type=F32)
+            s = jax.nn.sigmoid(gate)
+            both[f, here] = (hidden * up * s * (1.0 + gate * (1.0 - s))).astype(BF16)
+            both[f + ff // tile, here] = (hidden * gate * s).astype(BF16)
+        for n in range(dim // tile):
+            block = got[0, low:high, :, :, n * tile : (n + 1) * tile]
+            xt[n, :, here] = block.reshape(count, tile).T
+
+    def back_copy(part, j):
+        rows = pl.ds(0, 48) if part == 0 else pl.ds(48, 16)
+        return remote(
+            rows_back.at[j, rows], returned.at[j, rows],
+            b_send.at[part, j - 1], b_recv.at[part, j - 1], (rep, plane_exp(j)),
+        )
+
+    def row_grads(part):
+        low, high = ((0, 3), (3, 4))[part]
+        here, count = slice(low * 64, high * 64), (high - low) * 64
+
+        def one(n, carry):
+            cols = pl.ds(pl.multiple_of(n * tile, tile), tile)
+            total = jnp.zeros((count, tile), F32)
+            for k in range(ff // tile):
+                inner = slice(k * tile, (k + 1) * tile)
+                total += lax.dot_general(
+                    both[k, here], wg[cols, inner], over_last, preferred_element_type=F32
+                )
+                total += lax.dot_general(
+                    both[k + ff // tile, here], wu[cols, inner], over_last,
+                    preferred_element_type=F32,
+                )
+            value = total.astype(BF16).reshape(high - low, NJ, 16, tile)
+            for j in range(NJ):
+                rows = slice(low * 16, high * 16)
+                rows_back[j, rows, cols] = value[:, j].reshape(count // NJ, tile)
+            return carry
+
+        lax.fori_loop(0, dim // tile, one, 0)
+
+    def back_start(part):
+        for j in range(1, NJ):
+            copy = back_copy(part, j)
+            copy.start()
+            pending.append(copy)
 
     for hop in range(1, HALF + 1):
         for sub in range(SUBS):
@@ -163,39 +223,16 @@
                 if carries(way, hop, sub):
                     hop_copy(way, hop, sub).wait_recv()
                     hop_start(way, hop + 1, sub)
+        if hop == 2:
+            for copy in weights:
+                copy.wait()
         if hop % 2 == 0:
             select(hop // 2 - 1)
-
-    for copy in weights:
-        copy.wait()
-    for group in range(4):
-        for j in range(1, NJ):
-            for kind in range(2):
-                plane_copy(group, j, kind).wait_recv()
-
-    slots = NJ * 64
-    over_last = (((1,), (1,)), ((), ()))
-
-    def project(f, carry):
-        cols = pl.ds(pl.multiple_of(f * tile, tile), tile)
-        ins = got[0].reshape(slots, dim)
-        gate = jnp.dot(ins, wg[:, cols], preferred_element_type=F32)
-        up = jnp.dot(ins, wu[:, cols], preferred_element_type=F32)
-        grads = got[1].reshape(slots, dim)
-        hidden = lax.dot_general(grads, wd[cols, :], over_last, preferred_element_type=F32)
-        s = jax.nn.sigmoid(gate)
-        both[f] = (hidden * up * s * (1.0 + gate * (1.0 - s))).astype(BF16)
-        both[f + ff // tile] = (hidden * gate * s).astype(BF16)
-        return carry
-
-    lax.fori_loop(0, ff // tile, project, 0)
-
-    def turn(n, carry):
-        cols = pl.ds(pl.multiple_of(n * tile, tile), tile)
-        xt[n] = got[0, :, :, cols].reshape(slots, tile).T
-        return carry
-
-    lax.fori_loop(0, dim // tile, turn, 0)
+        elif hop == 5:
+            project(0, 2)
+    project(2, 3)
+    row_grads(0)
+    project(3, 4)
 
     axes = ((x_dev, y_dev), (y_dev, x_dev))
     order_of = [1 if p == 1 else 0 for p in range(pieces)]
@@ -203,7 +240,7 @@
     def weight_piece(p):
         order = order_of[p]
 
-        def one(i, carry):
+        for i in range(dim // tile):
             value = jnp.dot(xt[i], both[p], preferred_element_type=F32).astype(BF16)
             rx = (i // 2 - my_x + NX) % NX
             for h in range(2):
@@ -213,9 +250,6 @@
                     dw[p, rx, ry] = part
                 else:
                     dw[p, ry, rx] = part
-            return carry
-
-        lax.fori_loop(0, dim // tile, one, 0)
 
     def ring_copy(phase, p, way, m):
         to = axes[order_of[p]][phase](1 if way == 0 else -1)
@@ -279,37 +313,10 @@
         if phase == 0:
             ring_first(1, p)
 
-    def back_copy(j):
-        return remote(
-            rows_back.at[j], returned.at[j], b_send.at[j - 1], b_recv.at[j - 1],
-            (rep, plane_exp(j)),
-        )
-
-    def row_grads():
-        def one(n, carry):
-            cols = pl.ds(pl.multiple_of(n * tile, tile), tile)
-            total = jnp.zeros((slots, tile), F32)
-            for k in range(ff // tile):
-                inner = slice(k * tile, (k + 1) * tile)
-                total += lax.dot_general(
-                    both[k], wg[cols, inner], over_last, preferred_element_type=F32
-                )
-                total += lax.dot_general(
-                    both[k + ff // tile], wu[cols, inner], over_last, preferred_element_type=F32
-                )
-            value = total.astype(BF16).reshape(NJ, 64, tile)
-            rows_back[:, :, cols] = value
-            return carry
-
-        lax.fori_loop(0, dim // tile, one, 0)
-        for j in range(1, NJ):
-            copy = back_copy(j)
-            copy.start()
-            pending.append(copy)
-
     def combine():
-        for j in range(1, NJ):
-            back_copy(j).wait_recv()
+        for part in range(2):
+            for j in range(1, NJ):
+                back_copy(part, j).wait_recv()
         for group in range(3, -1, -1):
             rows = pl.ds(group * 16, 16)
             for n in range(0, dim, 512):
@@ -360,46 +367,43 @@
                 total = total + zrecv[way, 0, half].astype(F32)
             out_ref[:, cols] = total.astype(BF16)
 
+    do = functools.partial
     tasks = []
-    weight_piece(0)
-    ring_first(0, 0)
-    weight_piece(1)
-    ring_first(0, 1)
-    row_grads()
-    weight_piece(2)
-    ring_first(0, 2)
-    for p in range(3, pieces):
+    for p in range(pieces):
         weight_piece(p)
-
     x_pieces = [p for p in range(pieces) if order_of[p] == 0]
-    y_pieces = [p for p in range(pieces) if order_of[p] == 1]
-
-    def lot(p, follow):
-        ring_add(0, p)
-        if follow is not None:
-            ring_first(0, follow)
-
-    step = 7.9
+    ring_first(0, x_pieces[0])
+    for p in range(pieces):
+        if order_of[p] == 1:
+            ring_first(0, p)
+            tasks += [(10, do(ring_add, 0, p)), (26, do(ring_end, 0, p))]
+            tasks += [(34, do(ring_add, 1, p)), (42, do(ring_end, 1, p))]
+    back_start(0)
+    row_grads(1)
+    back_start(1)
+    step = 8.6
     for i, p in enumerate(x_pieces):
-        follow = x_pieces[i + 2] if i + 2 < len(x_pieces) else None
-        tasks.append((step * i + 4, functools.partial(lot, p, follow)))
-        tasks.append((step * (i + 1) + 2, functools.partial(ring_end, 0, p)))
-        tasks.append((step * (i + 1) + 5, functools.partial(ring_add, 1, p)))
-        tasks.append((step * (i + 1) + 9, functools.partial(ring_end, 1, p)))
-    for i, p in enumerate(y_pieces):
-        tasks.append((8.5, functools.partial(ring_add, 0, p)))
-        tasks.append((24, functools.partial(ring_end, 0, p)))
-        tasks.append((29, functools.partial(ring_add, 1, p)))
-        tasks.append((33, functools.partial(ring_end, 1, p)))
+        tasks.append((step * i + 5, do(ring_add, 0, p)))
+        if i + 1 < len(x_pieces):
+            tasks.append((step * i + 5.01, do(ring_first, 0, x_pieces[i + 1])))
+        tasks.append((step * (i + 1) + 6, do(ring_end, 0, p)))
+        tasks.append((step * (i + 1) + 12, do(ring_add, 1, p)))
+        tasks.append((step * (i + 1) + 20, do(ring_end, 1, p)))
     tasks.append((11, combine))
     tasks.append((11.1, line_far))
     for hop in range(HALF - 1, 0, -1):
-        tasks.append((11.2 + 3.5 * (HALF - hop), functools.partial(line_step, hop)))
-    tasks.append((11.2 + 3.5 * HALF, line_end))
+        tasks.append((11.2 + 5.3 * (HALF - hop), do(line_step, hop)))
+    tasks.append((11.2 + 5.3 * HALF, line_end))
     for _, task in sorted(tasks, key=lambda entry: entry[0]):
         task()
     for copy in pending:
         copy.wait_send()
+
+
+def hand_on(a, b, c, a_out, b_out, c_out):
+    a_out[...] = a[...]
+    b_out[...] = b[...]
+    c_out[...] = c[...]
 
 
 def body(quant_rows, row_scales, out_grads, routes, probs, w_gate, w_up, w_down):
@@ -428,7 +432,7 @@
             pltpu.VMEM((NZ, tok, dim), BF16),
             pltpu.VMEM((4, 64, NJ * tok), BF16),
             pltpu.VMEM((2, 4, NJ, 16, dim), BF16),
-            pltpu.VMEM((2, NJ, 64, dim), BF16),
+            pltpu.VMEM((2, 4, NJ, 16, dim), BF16),
             pltpu.VMEM((dim // 256, 256, 256), BF16),
             pltpu.VMEM((pieces, 256, 256), BF16),
             pltpu.VMEM((NJ, 64, dim), BF16),
@@ -445,8 +449,8 @@
             dma((2, HALF, SUBS)),
             dma((4, 3, 2)),
             dma((4, 3, 2)),
-            dma((3,)),
-            dma((3,)),
+            dma((2, 3)),
+            dma((2, 3)),
             dma((2, HALF, 2)),
             dma((2, HALF, 2)),
             dma((2, pieces, 2, 3)),
@@ -456,9 +460,15 @@
             collective_id=0, has_side_effects=True, vmem_limit_bytes=60 * 1024 * 1024
         ),
     )(
-        quant_rows, row_scales.reshape(1, tok), out_grads, routes, probs,
+        quant_rows, row_scales.reshape(1, tok), out_grads, routes.T, probs.T,
         w_gate[0], w_up[0], w_down[0],
     )
+    out, gate, up = pl.pallas_call(
+        hand_on,
+        out_shape=tuple(jax.ShapeDtypeStruct(a.shape, a.dtype) for a in (out, gate, up)),
+        in_specs=[vmem] * 3,
+        out_specs=(vmem,) * 3,
+    )(out, gate, up)
     return out, gate[None], up[None]
 
 

time: 167 us -> 159 us (0.952)
  local copies, waits for them, and re-layouts: 7.53 us -> 0 us
    unnamed x5 -> x0, local copies, waits for them, and re-layouts: 7.53 us -> none
    pallas_call x1, Pallas kernels: 157 us -> 154 us  [body(): pl.pallas_call(kernel, out_shape=(jax.ShapeDtypeStruct((tok, dim), BF16),...]
    pallas_call x0 -> x1, Pallas kernels: none -> 1.88 us  [body(): pl.pallas_call(hand_on, out_shape=tuple((jax.ShapeDtypeStruct(a.shape, a....]
where the time goes in v2:
time: 159 us; the launch traced here: 157 us
  Pallas kernels  156 us (98%)
    pallas_call x1, Pallas kernels, body(): pl.pallas_call(kernel, out_shape=(jax.ShapeDtypeStruct((tok, dim), BF16),...  154 us

profile of v2, /device:TPU:6, one launch (start us, length us, event | category | flops | bytes accessed | tf_op | source)
XLA Modules:
  0.0 156.5 jit_solution(1996849592574466937)
XLA Ops:
  0.6 154.0 %shard_map.103 = (bf16[32,2048]{1,0:T(8,128)(2,1)}, bf16[128,768]{1,0:T(8,128)(2,1)}, bf16[128,768]{1,0:T(8,128)(2,1)}) custom-call(bf16[32,2048]{1,0:T(8,128)(2,1)} %x_ref.1, bf16[1,32]{1,0:T(2,128)(2,1)} %bitcast.13, bf16[32,2048]{1,0:T(8,128)(2,1)} %g_ref.1, s32[4,32]{1,0:T(4,128)} %bitcast.11, bf16[4,32]{1,0:T(4,128)(2,1)} %bitcast.12, ...), custom_call_target="tpu_custom_call" | custom-call | tf_op jit(solution)/shard_map/pallas_call | solution.py:417
  154.7 1.9 %shard_map.104 = (bf16[32,2048]{1,0:T(8,128)(2,1)}, bf16[128,768]{1,0:T(8,128)(2,1)}, bf16[128,768]{1,0:T(8,128)(2,1)}) custom-call(bf16[32,2048]{1,0:T(8,128)(2,1)} %get-tuple-element.9.a, bf16[128,768]{1,0:T(8,128)(2,1)} %get-tuple-element.10.b, bf16[128,768]{1,0:T(8,128)(2,1)} %get-tuple-element.11.c), custom_call_target="tpu_custom_call" | custom-call | tf_op jit(solution)/shard_map/pallas_call | solution.py:466

commit v3 on v2

--- a/solution.py
+++ b/solution.py
@@ -160,12 +160,17 @@
     slots = NJ * 64
     over_last = (((1,), (1,)), ((), ()))
 
-    def project(low, high):
+    def project(low, high, arrived=None, ready=None):
         for group in range(low, high):
             for j in range(1, NJ):
                 for kind in range(2):
                     plane_copy(group, j, kind).wait_recv()
+        if arrived is not None:
+            arrived()
         here, count = slice(low * 64, high * 64), (high - low) * 64
+        for n in range(dim // tile):
+            block = got[0, low:high, :, :, n * tile : (n + 1) * tile]
+            xt[n, :, here] = block.reshape(count, tile).T
         for f in range(ff // tile):
             cols = slice(f * tile, (f + 1) * tile)
             ins = got[0, low:high].reshape(count, dim)
@@ -176,9 +181,8 @@
             s = jax.nn.sigmoid(gate)
             both[f, here] = (hidden * up * s * (1.0 + gate * (1.0 - s))).astype(BF16)
             both[f + ff // tile, here] = (hidden * gate * s).astype(BF16)
-        for n in range(dim // tile):
-            block = got[0, low:high, :, :, n * tile : (n + 1) * tile]
-            xt[n, :, here] = block.reshape(count, tile).T
+            if ready is not None:
+                ready(f)
 
     def back_copy(part, j):
         rows = pl.ds(0, 48) if part == 0 else pl.ds(48, 16)
@@ -232,10 +236,10 @@
             project(0, 2)
     project(2, 3)
     row_grads(0)
-    project(3, 4)
 
     axes = ((x_dev, y_dev), (y_dev, x_dev))
-    order_of = [1 if p == 1 else 0 for p in range(pieces)]
+    thirds = ff // tile
+    order_of = [1 if p == thirds else 0 for p in range(pieces)]
 
     def weight_piece(p):
         order = order_of[p]
@@ -269,10 +273,13 @@
         copy.start()
         pending.append(copy)
 
+    def ring_send(phase, p, m):
+        for way in range(2):
+            ring_start(phase, p, way, m)
+
     def ring_first(phase, p):
         for m in range(2):
-            for way in range(2):
-                ring_start(phase, p, way, m)
+            ring_send(phase, p, m)
 
     def ring_add(phase, p):
         for way in range(2):
@@ -368,32 +375,40 @@
             out_ref[:, cols] = total.astype(BF16)
 
     do = functools.partial
-    tasks = []
-    for p in range(pieces):
-        weight_piece(p)
-    x_pieces = [p for p in range(pieces) if order_of[p] == 0]
-    ring_first(0, x_pieces[0])
-    for p in range(pieces):
-        if order_of[p] == 1:
-            ring_first(0, p)
-            tasks += [(10, do(ring_add, 0, p)), (26, do(ring_end, 0, p))]
-            tasks += [(34, do(ring_add, 1, p)), (42, do(ring_end, 1, p))]
-    back_start(0)
+    y_piece = thirds
+    x_pieces = [p + half * thirds for p in range(thirds) for half in range(2)]
+    x_pieces.remove(y_piece)
+
+    def ready(f):
+        weight_piece(f)
+        if f == 0:
+            ring_first(0, x_pieces[0])
+        elif f == 1:
+            ring_send(0, x_pieces[1], 0)
+        weight_piece(f + thirds)
+
+    project(3, 4, do(back_start, 0), ready)
     row_grads(1)
     back_start(1)
+    ring_first(0, y_piece)
     step = 8.6
+    tasks = [(26, do(ring_add, 0, y_piece)), (42, do(ring_end, 0, y_piece))]
+    tasks += [(48, do(ring_add, 1, y_piece)), (54, do(ring_end, 1, y_piece))]
     for i, p in enumerate(x_pieces):
-        tasks.append((step * i + 5, do(ring_add, 0, p)))
+        when = step * i + 5
+        tasks.append((when, do(ring_add, 0, p)))
         if i + 1 < len(x_pieces):
-            tasks.append((step * i + 5.01, do(ring_first, 0, x_pieces[i + 1])))
-        tasks.append((step * (i + 1) + 6, do(ring_end, 0, p)))
-        tasks.append((step * (i + 1) + 12, do(ring_add, 1, p)))
-        tasks.append((step * (i + 1) + 20, do(ring_end, 1, p)))
-    tasks.append((11, combine))
-    tasks.append((11.1, line_far))
+            tasks.append((when + 0.01, do(ring_send, 0, x_pieces[i + 1], 1)))
+        if i + 2 < len(x_pieces):
+            tasks.append((when + 0.02, do(ring_send, 0, x_pieces[i + 2], 0)))
+        tasks.append((when + 9.6, do(ring_end, 0, p)))
+        tasks.append((when + 15.6, do(ring_add, 1, p)))
+        tasks.append((when + 23.6, do(ring_end, 1, p)))
+    tasks.append((16, combine))
+    tasks.append((16.1, line_far))
     for hop in range(HALF - 1, 0, -1):
-        tasks.append((11.2 + 5.3 * (HALF - hop), do(line_step, hop)))
-    tasks.append((11.2 + 5.3 * HALF, line_end))
+        tasks.append((16.2 + 4.6 * (HALF - hop), do(line_step, hop)))
+    tasks.append((16.2 + 4.6 * HALF, line_end))
     for _, task in sorted(tasks, key=lambda entry: entry[0]):
         task()
     for copy in pending:

time: 159 us -> 144 us (0.906); the launches traced: 157 us -> 144 us
  Pallas kernels: 156 us -> 143 us
    pallas_call x1, Pallas kernels: 154 us -> 141 us  [body(): pl.pallas_call(kernel, out_shape=(jax.ShapeDtypeStruct((tok, dim), BF16),...]
where the time goes in v3:
time: 144 us
  Pallas kernels  143 us (99%)
    pallas_call x1, Pallas kernels, body(): pl.pallas_call(kernel, out_shape=(jax.ShapeDtypeStruct((tok, dim), BF16),...  141 us

profile of v3, /device:TPU:6, one launch (start us, length us, event | category | flops | bytes accessed | tf_op | source)
XLA Modules:
  0.0 143.6 jit_solution(16425761305453660857)
XLA Ops:
  0.6 141.1 %shard_map.103 = (bf16[32,2048]{1,0:T(8,128)(2,1)}, bf16[128,768]{1,0:T(8,128)(2,1)}, bf16[128,768]{1,0:T(8,128)(2,1)}) custom-call(bf16[32,2048]{1,0:T(8,128)(2,1)} %x_ref.1, bf16[1,32]{1,0:T(2,128)(2,1)} %bitcast.13, bf16[32,2048]{1,0:T(8,128)(2,1)} %g_ref.1, s32[4,32]{1,0:T(4,128)} %bitcast.11, bf16[4,32]{1,0:T(4,128)(2,1)} %bitcast.12, ...), custom_call_target="tpu_custom_call" | custom-call | tf_op jit(solution)/shard_map/pallas_call | solution.py:432
  141.7 1.9 %shard_map.104 = (bf16[32,2048]{1,0:T(8,128)(2,1)}, bf16[128,768]{1,0:T(8,128)(2,1)}, bf16[128,768]{1,0:T(8,128)(2,1)}) custom-call(bf16[32,2048]{1,0:T(8,128)(2,1)} %get-tuple-element.9.a, bf16[128,768]{1,0:T(8,128)(2,1)} %get-tuple-element.10.b, bf16[128,768]{1,0:T(8,128)(2,1)} %get-tuple-element.11.c), custom_call_target="tpu_custom_call" | custom-call | tf_op jit(solution)/shard_map/pallas_call | solution.py:481

commit v4 on v3

--- a/solution.py
+++ b/solution.py
@@ -22,8 +22,9 @@
     x_ref, scale_ref, g_ref, routes_ref, probs_ref, wg_hbm, wu_hbm, wd_hbm,
     out_ref, gate_ref, up_ref,
     wg, wu, wd, meta, xs, gs, pm, stage, got, xt, both, rows_back, returned, yown,
-    zsend, zrecv, dw, zed, recv1, recv2,
+    zsend, zrecv, dw, zed, recv1, recv2, far_send, far_recv,
     w_sem, f_send, f_recv, p_send, p_recv, b_send, b_recv, z_send, z_recv, r_send, r_recv,
+    q_send, q_recv,
 ):
     tok, dim = x_ref.shape
     ff = wg.shape[1]
@@ -65,8 +66,8 @@
 
     diag = jnp.where(iota((tok, tok), 0) == iota((tok, tok), 1), scale_ref[...].astype(F32), 0.0)
     diag = diag.astype(BF16)
-    xs[0] = jnp.dot(diag, x_ref[...], preferred_element_type=F32).astype(BF16)
-    gs[0] = g_ref[...]
+    xs[12] = jnp.dot(diag, x_ref[...], preferred_element_type=F32).astype(BF16)
+    gs[12] = g_ref[...]
     lanes = NJ * tok
     spread = (iota((tok, lanes), 1) % tok == iota((tok, lanes), 0)).astype(BF16)
     over_tokens = (((0,), (0,)), ((), ()))
@@ -82,8 +83,8 @@
     rank = jnp.dot(named.astype(BF16), before, preferred_element_type=F32)
     for k in range(4):
         mine = jnp.sum(jnp.where(hits[k], rank, 0.0), axis=0, keepdims=True)
-        meta[0, k : k + 1, :] = table[k : k + 1] * CAP + mine
-        meta[0, 4 + k : 5 + k, :] = chance[k : k + 1]
+        meta[12, k : k + 1, :] = table[k : k + 1] * CAP + mine
+        meta[12, 4 + k : 5 + k, :] = chance[k : k + 1]
 
     pl.semaphore_wait(barrier, len(neighbours))
 
@@ -98,7 +99,8 @@
     travels = (meta, xs, gs)
 
     def slot_of(way, hop):
-        return 0 if hop == 0 else 15 if hop == HALF else 2 * hop - 1 + way
+        near = {0: 12, 1: 13 + way, HALF: 15}
+        return near[hop] if hop in near else 2 * (hop - 2) + way
 
     def carries(way, hop, sub):
         return hop < HALF or (sub == 2) == (way == 1)
@@ -136,26 +138,93 @@
             p_send.at[group, j - 1, kind], p_recv.at[group, j - 1, kind], (rep, plane_exp(j)),
         )
 
-    def select(group):
+    def picks(group):
         lane_group = iota((8, lanes), 1) // tok
         mix = meta[group * 4]
         for m in range(1, 4):
             mix = jnp.where(lane_group == m, meta[group * 4 + m], mix)
         hit = [slot_id == mix[k : k + 1] for k in range(4)]
         ones = sum(h.astype(F32) for h in hit)
-        pm[group] = ones.astype(BF16)
         weighed = sum(jnp.where(hit[k], mix[4 + k : 5 + k], 0.0) for k in range(4))
-        picks = (pm[group], weighed.astype(BF16))
-        for kind, buf in ((0, xs), (1, gs)):
-            for n in range(0, dim, 512):
-                block = buf[group * 4 : group * 4 + 4, :, n : n + 512].reshape(4 * tok, 512)
-                chosen = jnp.dot(picks[kind], block, preferred_element_type=F32).astype(BF16)
-                got[kind, group, 0, :, n : n + 512] = chosen[:16]
-                stage[kind, group, 1:, :, n : n + 512] = chosen[16:].reshape(3, 16, 512)
+        return ones.astype(BF16), weighed.astype(BF16)
+
+    def select(group, kind):
+        members = 4 if group < 3 else 3
+        pick = picks(group)
+        if kind == 0:
+            pm[group] = pick[0]
+        chosen_of = pick[kind][:, : members * tok]
+        buf = travels[1 + kind]
+        for n in range(0, dim, 512):
+            block = buf[group * 4 : group * 4 + members, :, n : n + 512]
+            block = block.reshape(members * tok, 512)
+            chosen = jnp.dot(chosen_of, block, preferred_element_type=F32).astype(BF16)
+            got[kind, group, 0, :, n : n + 512] = chosen[:16]
+            stage[kind, group, 1:, :, n : n + 512] = chosen[16:].reshape(3, 16, 512)
+        for j in range(1, NJ):
+            copy = plane_copy(group, j, kind)
+            copy.start()
+            pending.append(copy)
+
+    quarter = dim // 4
+
+    def far_copy(j, kind):
+        return remote(
+            far_send.at[kind, j - 1], far_recv.at[kind, j - 1],
+            q_send.at[j - 1, kind], q_recv.at[j - 1, kind], (rep, plane_exp(j)),
+        )
+
+    def far_picks(slot):
+        last = meta[15][:, :tok]
+        hit = [slot == last[k : k + 1] for k in range(4)]
+        ones = sum(h.astype(F32) for h in hit)
+        weighed = sum(jnp.where(hit[k], last[4 + k : 5 + k], 0.0) for k in range(4))
+        return ones, weighed
+
+    def select_far():
+        pm[3] = picks(3)[0]
+        row = iota((48, tok), 0)
+        owner = jnp.where(
+            row // 16 == 0, plane_exp(1), jnp.where(row // 16 == 1, plane_exp(2), plane_exp(3))
+        )
+        sent = far_picks((owner * CAP + row % CAP).astype(F32))
+        for kind in range(2):
+            buf = travels[1 + kind]
+            total = jnp.zeros((48, quarter), F32)
+            for q in range(4):
+                pick = jnp.where(row % 16 // CAP == q, sent[kind], 0.0).astype(BF16)
+                block = buf[15, :, q * quarter : (q + 1) * quarter]
+                total += jnp.dot(pick, block, preferred_element_type=F32)
+            far_send[kind] = total.astype(BF16).reshape(3, 16, quarter)
             for j in range(1, NJ):
-                copy = plane_copy(group, j, kind)
+                copy = far_copy(j, kind)
                 copy.start()
                 pending.append(copy)
+        row = iota((16, tok), 0)
+        slot = jnp.where(row // CAP == 3, plane_exp(0) * CAP + row % CAP, -1)
+        kept = far_picks(slot.astype(F32))
+        for kind in range(2):
+            buf = travels[1 + kind]
+            for n in range(0, dim, 512):
+                cols = slice(n, n + 512)
+                more = jnp.dot(
+                    kept[kind].astype(BF16), buf[15, :, cols], preferred_element_type=F32
+                )
+                got[kind, 3, 0, :, cols] = (got[kind, 3, 0, :, cols].astype(F32) + more).astype(BF16)
+
+    def unpack_far():
+        a, b = iota((48, 48), 0), iota((48, 48), 1)
+        same = (a // 16 == b // 16) & (a % 16 // CAP == 3) & (a % CAP == b % CAP)
+        for kind in range(2):
+            for j in range(1, NJ):
+                far_copy(j, kind).wait_recv()
+            packed = far_recv[kind].reshape(48, quarter)
+            for q in range(4):
+                cols = slice(q * quarter, (q + 1) * quarter)
+                place = (same & (b % 16 // CAP == q)).astype(F32).astype(BF16)
+                more = jnp.dot(place, packed, preferred_element_type=F32)
+                old = got[kind, 3, 1:, :, cols].reshape(48, quarter).astype(F32)
+                got[kind, 3, 1:, :, cols] = (old + more).astype(BF16).reshape(3, 16, quarter)
 
     slots = NJ * 64
     over_last = (((1,), (1,)), ((), ()))
@@ -185,14 +254,14 @@
                 ready(f)
 
     def back_copy(part, j):
-        rows = pl.ds(0, 48) if part == 0 else pl.ds(48, 16)
+        rows = pl.ds(part * 32, 32)
         return remote(
             rows_back.at[j, rows], returned.at[j, rows],
             b_send.at[part, j - 1], b_recv.at[part, j - 1], (rep, plane_exp(j)),
         )
 
     def row_grads(part):
-        low, high = ((0, 3), (3, 4))[part]
+        low, high = ((0, 2), (2, 4))[part]
         here, count = slice(low * 64, high * 64), (high - low) * 64
 
         def one(n, carry):
@@ -221,20 +290,21 @@
             copy.start()
             pending.append(copy)
 
+    group_at = {1: 3, 3: 0, 5: 1, 7: 2}
     for hop in range(1, HALF + 1):
         for sub in range(SUBS):
             for way in range(2):
                 if carries(way, hop, sub):
                     hop_copy(way, hop, sub).wait_recv()
                     hop_start(way, hop + 1, sub)
+            if hop in group_at and sub > 0:
+                select(group_at[hop], sub - 1)
         if hop == 2:
             for copy in weights:
                 copy.wait()
-        if hop % 2 == 0:
-            select(hop // 2 - 1)
-        elif hop == 5:
-            project(0, 2)
-    project(2, 3)
+        if hop >= 6 and hop < HALF:
+            project(hop - 6, hop - 5)
+    select_far()
     row_grads(0)
 
     axes = ((x_dev, y_dev), (y_dev, x_dev))
@@ -368,7 +438,7 @@
     def line_end():
         for half in range(2):
             cols = slice(half * wide, (half + 1) * wide)
-            total = yown[0, :, cols]
+            total = yown[12, :, cols]
             for way in range(2):
                 line_copy(way, 1, half).wait_recv()
                 total = total + zrecv[way, 0, half].astype(F32)
@@ -387,7 +457,11 @@
             ring_send(0, x_pieces[1], 0)
         weight_piece(f + thirds)
 
-    project(3, 4, do(back_start, 0), ready)
+    def arrived():
+        unpack_far()
+        back_start(0)
+
+    project(2, 4, arrived, ready)
     row_grads(1)
     back_start(1)
     ring_first(0, y_piece)
@@ -459,6 +533,8 @@
             pltpu.VMEM((pieces, 4, 128, 256), BF16),
             pltpu.VMEM((pieces, 2, 3, 2, 128, 256), BF16),
             pltpu.VMEM((pieces, 2, 3, 64, 256), BF16),
+            pltpu.VMEM((2, 3, 16, dim // 4), BF16),
+            pltpu.VMEM((2, 3, 16, dim // 4), BF16),
             dma((3,)),
             dma((2, HALF, SUBS)),
             dma((2, HALF, SUBS)),
@@ -470,6 +546,8 @@
             dma((2, HALF, 2)),
             dma((2, pieces, 2, 3)),
             dma((2, pieces, 2, 3)),
+            dma((3, 2)),
+            dma((3, 2)),
         ],
         compiler_params=pltpu.CompilerParams(
             collective_id=0, has_side_effects=True, vmem_limit_bytes=60 * 1024 * 1024

time: 144 us -> 145 us (level); the launches traced: 144 us -> 143 us
  no operation moved by 1% of the time
where the time goes in v4:
time: 145 us; the launch traced here: 143 us
  Pallas kernels  142 us (98%)
    pallas_call x1, Pallas kernels, body(): pl.pallas_call(kernel, out_shape=(jax.ShapeDtypeStruct((tok, dim), BF16),...  140 us

profile of v4, /device:TPU:6, one launch (start us, length us, event | category | flops | bytes accessed | tf_op | source)
XLA Modules:
  0.0 142.6 jit_solution(12064715798183768338)
XLA Ops:
  0.6 140.1 %shard_map.103 = (bf16[32,2048]{1,0:T(8,128)(2,1)}, bf16[128,768]{1,0:T(8,128)(2,1)}, bf16[128,768]{1,0:T(8,128)(2,1)}) custom-call(bf16[32,2048]{1,0:T(8,128)(2,1)} %x_ref.1, bf16[1,32]{1,0:T(2,128)(2,1)} %bitcast.13, bf16[32,2048]{1,0:T(8,128)(2,1)} %g_ref.1, s32[4,32]{1,0:T(4,128)} %bitcast.11, bf16[4,32]{1,0:T(4,128)(2,1)} %bitcast.12, ...), custom_call_target="tpu_custom_call" | custom-call | tf_op jit(solution)/shard_map/pallas_call | solution.py:506
  140.8 1.9 %shard_map.104 = (bf16[32,2048]{1,0:T(8,128)(2,1)}, bf16[128,768]{1,0:T(8,128)(2,1)}, bf16[128,768]{1,0:T(8,128)(2,1)}) custom-call(bf16[32,2048]{1,0:T(8,128)(2,1)} %get-tuple-element.9.a, bf16[128,768]{1,0:T(8,128)(2,1)} %get-tuple-element.10.b, bf16[128,768]{1,0:T(8,128)(2,1)} %get-tuple-element.11.c), custom_call_target="tpu_custom_call" | custom-call | tf_op jit(solution)/shard_map/pallas_call | solution.py:559

commit v5 on v4

--- a/solution.py
+++ b/solution.py
@@ -478,11 +478,11 @@
         tasks.append((when + 9.6, do(ring_end, 0, p)))
         tasks.append((when + 15.6, do(ring_add, 1, p)))
         tasks.append((when + 23.6, do(ring_end, 1, p)))
-    tasks.append((16, combine))
-    tasks.append((16.1, line_far))
+    tasks.append((20, combine))
+    tasks.append((20.1, line_far))
     for hop in range(HALF - 1, 0, -1):
-        tasks.append((16.2 + 4.6 * (HALF - hop), do(line_step, hop)))
-    tasks.append((16.2 + 4.6 * HALF, line_end))
+        tasks.append((20.2 + 4.2 * (HALF - hop), do(line_step, hop)))
+    tasks.append((20.2 + 4.2 * HALF, line_end))
     for _, task in sorted(tasks, key=lambda entry: entry[0]):
         task()
     for copy in pending:

time: 145 us -> 145 us (level); the launches traced: 143 us -> 144 us
  Pallas kernels: 142 us -> 144 us
    pallas_call x1, Pallas kernels: 140 us -> 142 us  [body(): pl.pallas_call(kernel, out_shape=(jax.ShapeDtypeStruct((tok, dim), BF16),...]
where the time goes in v5:
time: 145 us; the launch traced here: 144 us
  Pallas kernels  144 us (99%)
    pallas_call x1, Pallas kernels, body(): pl.pallas_call(kernel, out_shape=(jax.ShapeDtypeStruct((tok, dim), BF16),...  142 us

profile of v5, /device:TPU:6, one launch (start us, length us, event | category | flops | bytes accessed | tf_op | source)
XLA Modules:
  0.0 144.5 jit_solution(6014199346782704123)
XLA Ops:
  0.6 142.0 %shard_map.103 = (bf16[32,2048]{1,0:T(8,128)(2,1)}, bf16[128,768]{1,0:T(8,128)(2,1)}, bf16[128,768]{1,0:T(8,128)(2,1)}) custom-call(bf16[32,2048]{1,0:T(8,128)(2,1)} %x_ref.1, bf16[1,32]{1,0:T(2,128)(2,1)} %bitcast.13, bf16[32,2048]{1,0:T(8,128)(2,1)} %g_ref.1, s32[4,32]{1,0:T(4,128)} %bitcast.11, bf16[4,32]{1,0:T(4,128)(2,1)} %bitcast.12, ...), custom_call_target="tpu_custom_call" | custom-call | tf_op jit(solution)/shard_map/pallas_call | solution.py:506
  142.6 1.9 %shard_map.104 = (bf16[32,2048]{1,0:T(8,128)(2,1)}, bf16[128,768]{1,0:T(8,128)(2,1)}, bf16[128,768]{1,0:T(8,128)(2,1)}) custom-call(bf16[32,2048]{1,0:T(8,128)(2,1)} %get-tuple-element.9.a, bf16[128,768]{1,0:T(8,128)(2,1)} %get-tuple-element.10.b, bf16[128,768]{1,0:T(8,128)(2,1)} %get-tuple-element.11.c), custom_call_target="tpu_custom_call" | custom-call | tf_op jit(solution)/shard_map/pallas_call | solution.py:559
